TPU v7x, 32 devices: a whole 2x2x4 slice. The times are simulated.
32 devices in a mesh: dp: 8 (over z, y), mp: 4 (over x, core).
Axes of the slice: x: 2, y: 2, z: 4, core: 2. Of those that a mesh axis runs over, the one named last changes fastest.
Arguments:
- features: bfloat16 [9216, 1024], P('dp'), may hold values from -6 to 6
- stem_weight: bfloat16 [1024, 1024], P(None, 'mp'), may hold values from -0.1875 to 0.1875
- group_gain: float32 [1024], P('mp'), may hold values from 0.1 to 1.9
- group_bias: float32 [1024], P('mp'), may hold values from -3 to 3
- embed_weight: bfloat16 [1024, 768], P('mp'), may hold values from -0.1875 to 0.1875
- first_gain: float32 [768], replicated, may hold values from 0.1 to 1.9
- first_bias: float32 [768], replicated, may hold values from -2 to 2
- project_in: bfloat16 [768, 2304], P(None, 'mp'), may hold values from -0.21875 to 0.21875
- project_out: bfloat16 [768, 768], P('mp'), may hold values from -3 to 3
- second_gain: float32 [768], replicated, may hold values from 0.1 to 1.9
- second_bias: float32 [768], replicated, may hold values from -2 to 2
- up_weight: bfloat16 [768, 3072], P(None, 'mp'), may hold values from -0.21875 to 0.21875
- up_bias: float32 [3072], P('mp'), may hold values from -3 to 3
- down_weight: bfloat16 [3072, 768], P('mp'), may hold values from -0.109375 to 0.109375
- valid_mask: int32 [16, 576], replicated, may hold values from 0 to 1, as said below
- slot_slice: int32 [16], P('dp'), may hold values from 0 to 15, each once
- cotangent: bfloat16 [9216, 768], P(('dp', 'mp')), may hold values from -6 to 6
Outputs:
- block_out: bfloat16 [9216, 768], P(('dp', 'mp'))
- features_grad: float32 [9216, 1024], P(('dp', 'mp'))
- stem_weight_grad: float32 [1024, 1024], P(None, 'mp')
- group_gain_grad: float32 [1024], P('mp')
- group_bias_grad: float32 [1024], P('mp')
- embed_weight_grad: float32 [1024, 768], P('mp')
- first_gain_grad: float32 [768], replicated
- first_bias_grad: float32 [768], replicated
- project_in_grad: float32 [768, 2304], P(None, 'mp')
- project_out_grad: float32 [768, 768], P('mp')
- second_gain_grad: float32 [768], replicated
- second_bias_grad: float32 [768], replicated
- up_weight_grad: float32 [768, 3072], P(None, 'mp')
- up_bias_grad: float32 [3072], P('mp')
- down_weight_grad: float32 [3072, 768], P('mp')
Inputs may be any that keep to these rules, and one draw needn't show every extreme that they name: `valid_mask`: row s is 1 at the positions below slice s's valid length, 196 or 576, and 0 after; half of the slices have each length. `slot_slice`: each slice stands in exactly one slot; slots j * 2 to (j + 1) * 2 - 1 are on index j of dp.
All inputs are finite; a program needn't handle non-finite values.
Results may differ from a plain program's by a relative error of at most 0.019.
Values may be sent and summed in bfloat16 or wider, within the bound.
A program may use at most 128 MiB of HBM per device.

v0:
```python
import functools
import itertools

import jax
import jax.numpy as jnp
from jax import lax
from jax.experimental import pallas as pl
from jax.experimental.pallas import tpu as pltpu
from jax.sharding import PartitionSpec as P

MESH = pl.DeviceIdType.MESH
F32 = jnp.float32
BF16 = jnp.bfloat16
HEAD_DIM = 64
GROUP = 32
NEAR = 8


def dot(left, right, left_dim=1, right_dim=0, precision=None):
    return lax.dot_general(
        left,
        right,
        (((left_dim,), (right_dim,)), ((), ())),
        precision=precision,
        preferred_element_type=F32,
    )


def gelu_parts(z):
    cdf = 0.5 + 0.5 * lax.erf(z * 0.7071067811865476)
    return z * cdf, cdf + z * (jnp.exp(-0.5 * z * z) * 0.3989422804014327)


class Net:
    def __init__(self, place, send_sems, recv_sems, local_sems):
        self.place = place
        self.send_sems, self.recv_sems, self.local_sems = send_sems, recv_sems, local_sems
        self.count, self.local_count, self.unsent = 0, 0, []

    def by(self, who, action):
        if who is None:
            action()
        else:
            pl.when(self.place.inner if who else jnp.logical_not(self.place.inner))(action)

    def plan(self, src, dst, device, who=None):
        copy = pltpu.make_async_remote_copy(
            src_ref=src,
            dst_ref=dst,
            send_sem=self.send_sems.at[self.count],
            recv_sem=self.recv_sems.at[self.count],
            device_id=device,
            device_id_type=MESH,
        )
        self.count += 1
        self.unsent.append((copy, who))
        return copy

    def send(self, src, dst, device, who=None):
        copy = self.plan(src, dst, device, who)
        self.by(who, copy.start)
        return copy

    def sent(self, copy):
        self.unsent = [one for one in self.unsent if one[0] is not copy]
        copy.wait_send()

    def local(self, src, dst, who=None):
        copy = pltpu.make_async_copy(src, dst, self.local_sems.at[self.local_count])
        self.local_count += 1
        self.by(who, copy.start)
        return copy

    def finish(self):
        for copy, who in self.unsent:
            self.by(who, copy.wait_send)


class Summed:
    def __init__(self, net, place, away, back, grad, arrive, out):
        self.net, self.place, self.away, self.back = net, place, away, back
        self.grad, self.arrive, self.out = grad, arrive, out
        self.dims = "xyb"[3 - (len(grad.shape) - 2) :]
        self.fixed = {}
        self.level, self.gathered = 0, None

    def index(self, dims, **more):
        fixed = {**self.fixed, **more}
        return tuple(pl.ds(fixed[dim], 1) if dim in fixed else pl.ds(0, 2) for dim in dims)

    def start(self):
        dim = self.away[self.level]
        bit, partner = self.place.partner(dim)
        inner_only = "a" in self.away[: self.level]
        if dim == "a":
            give, who = self.index(self.dims), False
        else:
            give, who = self.index(self.dims, **{dim: 1 - bit}), True if inner_only else None
            self.fixed[dim] = bit
        self.copy = self.net.send(self.grad.at[give], self.arrive[self.level], partner, who)

    def add(self, arrived):
        for at in itertools.product((0, 1), repeat=len(self.dims)):
            here = dict(zip(self.dims, at))
            if any(here[dim] for dim in self.fixed):
                continue
            where = tuple(self.fixed.get(dim, here[dim]) for dim in self.dims)
            value = self.grad[where].astype(F32) + arrived[at].astype(F32)
            self.grad[where] = value.astype(BF16)

    def held(self):
        return self.out.at[self.index("yb")]

    def share(self):
        dim = self.back[len(self.gathered)]
        _, partner = self.place.partner(dim)
        source = self.held()
        if not self.gathered:
            at = self.index("yb")
            source = self.grad.at[(0,) + at if "x" in self.dims else at]
        self.copy = self.net.send(source, self.held(), partner, True)
        if dim == "a" and len(self.gathered) < 2:
            _, partner = self.place.partner(self.back[2])
            self.last = self.net.plan(self.held(), self.held(), partner)
            self.net.by(True, self.last.start)

    def step(self):
        copy = self.copy
        if self.gathered is None:
            arrived = self.arrive[self.level]

            def take():
                copy.wait_recv()
                self.add(arrived)

            self.net.by(True if "a" in self.away[: self.level + 1] else None, take)
            self.level += 1
            if self.level < len(self.away):
                self.start()
                return
            self.fixed.pop("x", None)
            self.gathered = []
            at = self.index("yb")
            source = self.grad.at[(0,) + at if "x" in self.dims else at]
            self.own = self.net.local(source, self.held(), True)
            self.share()
            return
        dim = self.back[len(self.gathered)]
        if dim == "a":
            self.net.by(False, copy.wait_recv)
        elif "a" in self.gathered:
            copy.wait_recv()
        else:
            self.net.by(True, copy.wait_recv)
        if not self.gathered:
            self.net.by(True, self.own.wait)
        self.gathered.append(dim)
        self.fixed.pop(dim, None)
        if len(self.gathered) == 3:
            self.copy = None
        elif dim == "a":
            self.copy = self.last
            self.net.by(False, self.copy.start)
        else:
            self.share()

    def step_all(self):
        while self.copy is not None:
            self.step()


class Place:
    def __init__(self):
        self.d = lax.axis_index("dp")
        self.m = lax.axis_index("mp")
        self.x = lax.div(self.m, 2)
        self.c = lax.rem(self.m, 2)
        self.y = lax.rem(self.d, 2)
        self.zi = lax.div(lax.rem(self.d, NEAR), 2)
        self.sib_m = self.m + 1 - 2 * self.c
        self.far_m = lax.rem(self.m + 2, 4)
        self.far_sib_m = lax.rem(self.sib_m + 2, 4)
        self.sib = (self.d, self.sib_m)
        self.far = (self.d, self.far_m)
        self.y_device = (self.d + 1 - 2 * self.y, self.m)
        self.inner = jnp.logical_or(self.zi == 1, self.zi == 2)
        self.bits = {
            "y": (self.y, 1),
            "a": (lax.rem(self.zi, 2), 2),
            "b": (lax.div(self.zi, 2), 2),
            "w": (lax.div(self.zi, 2), 4),
        }

    def partner(self, name):
        if name == "x":
            return 0, self.far
        bit, stride = self.bits[name]
        return bit, (self.d + stride - 2 * stride * bit, self.m)


GRADS = ("up0", "up1", "down0", "down1", "pout", "pin0", "pin1", "pin2", "embed", "stem0", "stem1")
UP0, UP1, DOWN0, DOWN1, POUT, PIN0, PIN1, PIN2, EMBED, STEM0, STEM1, SMALL = range(12)
(NORM2, RESULT, MIXED_BACK, HEADS_FAR, HEADS_OWN, NORM1_SEND, NORM1, STEM_FAR, STEM_OWN, FEATURES_SEND,
 FEATURES_SUM) = range(12, 23)
KINDS = dict(g="grad", o="out", r0="arrive0", r1="arrive1", r2="arrive2", r3="arrive3")
AWAY = dict(
    down0="yab",
    down1="aby",
    up0="yab",
    up1="yab",
    pout="xaby",
    pin0="xaby",
    pin1="yxab",
    pin2="yxab",
    embed="xaby",
    stem0="xaby",
    stem1="xyab",
)
BACK = dict(
    down0="bay",
    down1="yba",
    up0="bay",
    up1="bay",
    pout="bay",
    pin0="bay",
    pin1="bay",
    pin2="bya",
    embed="bay",
    stem0="bay",
    stem1="bay",
)
ORDER = (
    NORM2, ~RESULT, DOWN0, MIXED_BACK, HEADS_FAR, ~POUT, DOWN1, UP0, HEADS_OWN, ~PIN1, DOWN0, UP1,
    NORM1_SEND, DOWN1, UP0, NORM1, ~PIN0, ~PIN2, POUT, DOWN0, STEM_FAR, ~STEM0, ~EMBED, PIN1, UP1,
    UP0, STEM_OWN, ~STEM1, DOWN1, DOWN0, FEATURES_SEND, SMALL, PIN0, POUT, UP1, FEATURES_SUM, PIN2,
    RESULT, UP0, STEM0, DOWN1, PIN0, POUT, DOWN0, UP1, STEM0, EMBED, UP0, PIN1, DOWN0, DOWN1, POUT,
    PIN0, UP1, STEM1, SMALL, EMBED, STEM0, UP0, POUT, PIN2, PIN1, PIN0, UP1, PIN2, EMBED, PIN1,
    STEM1, SMALL, DOWN1, STEM0, PIN0, PIN2, POUT, PIN1, EMBED, STEM0, SMALL, STEM1, PIN0, PIN2,
    POUT, PIN1, EMBED, STEM1, STEM0, PIN0, SMALL, STEM1, PIN1, PIN2, EMBED, STEM0, STEM1, EMBED,
    STEM1, PIN2,
)


def kernel(in_names, out_names, scratch_names, *refs):
    names = in_names + out_names + scratch_names
    r = dict(zip(names, refs))
    sums = {name: {} for name in GRADS}
    for name in names:
        kind, _, which = name.partition("_")
        if which in sums and kind in KINDS:
            sums[which][KINDS[kind]] = r.pop(name)
    for refs in sums.values():
        refs["arrive"] = [refs.pop(kind) for kind in sorted(refs) if kind.startswith("arrive")]
    run(sums=sums, **r)


def run(
    features, stem_weight, group_gain, group_bias, embed_weight, first_gain, first_bias,
    project_in, project_out, second_gain, second_bias, up_weight, up_bias, down_weight,
    valid_mask, slot_slice, cotangent,
    block_out, features_grad, o_small,
    feat, stem, std, wstat, embed, pin, pout, up, down, gvec, xhs, dgs, act, gst,
    sbuf, rbuf, res1, xh1, rs1, n1, q, k, v, probs, heads, mixed, res2, xh2, rs2,
    n2, hid, branch, preg, own, csend, crecv, xsend, xrecv, mb, pg,
    sm, smr, send_sems, recv_sems, local_sems, sums,
):
    place = Place()
    net = Net(place, send_sems, recv_sems, local_sems)
    x, c = place.x, place.c
    R = cotangent.shape[0]
    L = feat.shape[0]
    D = up.shape[0]
    own_rows = pl.multiple_of(c * R, 16)
    sib_rows = pl.multiple_of((1 - c) * R, 16)

    def block(m):
        return pl.ds(pl.multiple_of(m * R, 16), R)

    barrier = pltpu.get_barrier_semaphore()
    peers = [place.sib] + [place.partner(name)[1] for name in "xyaw"]
    for peer in peers:
        pl.semaphore_signal(barrier, inc=1, device_id=peer, device_id_type=MESH)

    def greet():
        peer = place.partner("b")[1]
        pl.semaphore_signal(barrier, inc=1, device_id=peer, device_id_type=MESH)

    net.by(True, greet)
    l_stem = net.local(stem_weight, stem.at[0])
    l_feat = net.local(features.at[pl.ds(pl.multiple_of(x * L, 16), L)], feat)
    l_embed = net.local(embed_weight, embed.at[0])
    l_cot = net.local(cotangent, branch.at[block(place.m)])
    l_pin = net.local(project_in, pin.at[0])
    l_pout = net.local(project_out, pout.at[0])
    l_up = net.local(up_weight, up)
    l_down = net.local(down_weight, down)
    gvec[0, 0:1, :] = group_gain[...].reshape(1, -1)
    gvec[0, 1:2, :] = group_bias[...].reshape(1, -1)
    pl.semaphore_wait(barrier, len(peers) + place.inner.astype(jnp.int32))

    c_gvec = net.send(gvec.at[0], gvec.at[1], place.far)

    def halves(weight, kept, pieces):
        rows = weight.shape[0] // pieces // 2
        for t in range(pieces):
            at = pl.ds(pl.multiple_of((2 * t + place.y) * rows, 16), rows)
            yield kept.at[1, at], net.send(weight.at[at], kept.at[1, at], place.far)

    stem_half = list(halves(stem_weight, stem, 2))
    embed_half = list(halves(embed_weight, embed, 1))
    pin_half = list(halves(project_in, pin, pin.shape[1] // (3 * HEAD_DIM)))
    pout_half = list(halves(project_out, pout, 1))
    c_cot = [
        net.send(cotangent, branch.at[block(place.m)], device) for device in (place.far, place.sib)
    ]

    def pass_on(half):
        ref, copy = half
        copy.wait_recv()
        return net.send(ref, ref, place.y_device)

    slices = valid_mask.shape[0]
    lengths = jnp.sum(valid_mask[...].astype(F32), axis=1, keepdims=True)
    mine = lax.broadcasted_iota(jnp.int32, (slices, 1), 0) == slot_slice[x]
    length = jnp.sum(jnp.where(mine, lengths, 0.0), axis=0, keepdims=True)

    def valid_rows(start, count):
        at = (lax.broadcasted_iota(jnp.int32, (count, 1), 0) + start).astype(F32)
        return jnp.where(at < length, 1.0, 0.0)

    key_valid = jnp.where(
        lax.broadcasted_iota(jnp.int32, (1, L), 1).astype(F32) < length, 1.0, 0.0
    )
    score_scale = HEAD_DIM ** (-0.5)
    key_scale = key_valid * score_scale
    key_shift = (key_valid - 1.0) * 1e9

    channels = stem.shape[2]
    same = (
        lax.div(lax.broadcasted_iota(jnp.int32, (channels, channels), 0), GROUP)
        == lax.div(lax.broadcasted_iota(jnp.int32, (channels, channels), 1), GROUP)
    )
    same = jnp.where(same, 1.0, 0.0)

    def group_sum(values):
        wide = jnp.broadcast_to(values, (8, channels))
        return dot(wide, same, precision=lax.Precision.HIGHEST)[0:1]

    def standardize(j):
        w = stem[j].astype(F32)
        average = jnp.sum(w, axis=0, keepdims=True) * (1.0 / w.shape[0])
        w = w - average
        scale = lax.rsqrt(jnp.sum(w * w, axis=0, keepdims=True) * (1.0 / w.shape[0]) + 1e-5)
        std[j] = (w * scale).astype(BF16)
        wstat[j, 0:1, :] = average
        wstat[j, 1:2, :] = scale

    tile_rows = [(t * R, R) for t in range(L // R)]

    def stem_forward(j):
        count = 1.0 / (length * GROUP)
        total = jnp.zeros((1, channels), F32)
        for at, size in tile_rows:
            s = dot(feat[at : at + size, :], std[j])
            xhs[j, at : at + size, :] = s
            total = total + jnp.sum(s * valid_rows(at, size), axis=0, keepdims=True)
        average = group_sum(total) * count
        total = jnp.zeros((1, channels), F32)
        for at, size in tile_rows:
            s = xhs[j, at : at + size, :] - average
            total = total + jnp.sum(s * s * valid_rows(at, size), axis=0, keepdims=True)
        scale = lax.rsqrt(group_sum(total) * count + 1e-5)
        gst[j, 0:1, :] = scale
        for at, size in tile_rows:
            xh = (xhs[j, at : at + size, :] - average) * scale
            xhs[j, at : at + size, :] = xh
            value, slope = gelu_parts(xh * gvec[j, 0:1, :] + gvec[j, 1:2, :])
            act[j, at : at + size, :] = value.astype(BF16)
            dgs[j, at : at + size, :] = slope

    l_stem.wait()
    standardize(0)
    c_stem = [pass_on(stem_half[0])]
    l_feat.wait()
    stem_forward(0)
    c_stem.append(pass_on(stem_half[1]))
    c_gvec.wait_recv()
    c_embed = pass_on(embed_half[0])
    for copy in c_stem:
        copy.wait_recv()
    standardize(1)
    stem_forward(1)
    l_embed.wait()
    c_embed.wait_recv()

    def core_sum(product):
        width = pl.ds(0, D)
        sbuf[:, width] = product(sib_rows)
        copy = net.send(sbuf.at[:, width], rbuf.at[:, width], place.sib)
        mine = product(own_rows)
        copy.wait_recv()
        net.sent(copy)
        return mine

    def embed_product(start):
        rows = pl.ds(start, R)
        return dot(act[0, rows, :], embed[0]) + dot(act[1, rows, :], embed[1])

    res1[...] = core_sum(embed_product)

    step = R // 3

    def layer_norm(res, other, add, gain, bias, xh_ref, scale_ref, out_ref, out_start):
        gain, bias = gain[...].reshape(1, -1), bias[...].reshape(1, -1)
        for t in range(3):
            rows = slice(t * step, (t + 1) * step)
            value = res[rows, :] + other[rows, 0:D]
            if add is not None:
                value = value + add[rows, :]
            res[rows, :] = value
            average = jnp.sum(value, axis=1, keepdims=True) * (1.0 / D)
            value = value - average
            scale = lax.rsqrt(jnp.sum(value * value, axis=1, keepdims=True) * (1.0 / D) + 1e-6)
            xh = value * scale
            xh_ref[rows, :] = xh
            scale_ref[rows, :] = scale
            out_ref[pl.ds(out_start + t * step, step), :] = (xh * gain + bias).astype(BF16)

    layer_norm(res1, rbuf, None, first_gain, first_bias, xh1, rs1, n1, own_rows)
    c_n1 = net.send(n1.at[pl.ds(own_rows, R)], n1.at[pl.ds(own_rows, R)], place.sib)
    l_pin.wait()
    c_n1.wait_recv()

    per_shard = pin.shape[1] // (3 * HEAD_DIM)

    width = 3 * HEAD_DIM
    pin_y = [net.plan(ref, ref, place.y_device) for ref, _ in pin_half]

    def pass_pin(i):
        pin_half[i][1].wait_recv()
        pin_y[i].start()

    def attend(h, carry):
        j, i = lax.div(h, per_shard), lax.rem(h, per_shard)
        for at in range(1, per_shard):

            @pl.when(h == at)
            def _():
                pass_pin(at)

        for at in range(per_shard):

            @pl.when(h == per_shard + at)
            def _():
                pin_y[at].wait_recv()

        @pl.when(h == per_shard + 1)
        def _():
            pout_half[0][1].wait_recv()
            pout_y.start()

        weight = pin[j, pl.ds(pl.multiple_of(i * width, 16), width), :]
        for at, size in tile_rows:
            packed = dot(n1[at : at + size, :], weight, 1, 1).astype(BF16)
            for t, ref in enumerate((q, k, v)):
                ref[h, at : at + size, :] = packed[:, t * HEAD_DIM : (t + 1) * HEAD_DIM]
        for at, size in tile_rows:
            s = dot(q[h, at : at + size, :], k[h], 1, 1) * key_scale + key_shift
            s = jnp.exp(s - jnp.max(s, axis=1, keepdims=True))
            p = (s * (1.0 / jnp.sum(s, axis=1, keepdims=True))).astype(BF16)
            probs[h, at : at + size, :] = p
            heads[h, at : at + size, :] = dot(p, v[h]).astype(BF16)
        return carry

    pass_pin(0)
    pout_y = net.plan(pout_half[0][0], pout_half[0][0], place.y_device)
    lax.fori_loop(0, 2 * per_shard, attend, 0)

    def side_by_side(pieces, store):
        at = 0
        while at < len(pieces):
            pair = pieces[at : at + 2]
            value = pair[0] if len(pair) == 1 else jnp.concatenate(pair, axis=1)
            store(slice(at * HEAD_DIM, at * HEAD_DIM + value.shape[1]), value)
            at += 2

    def store_mixed(lanes, value):
        mixed[:, lanes] = value

    side_by_side([heads[h] for h in range(2 * per_shard)], store_mixed)
    l_pout.wait()
    pout_y.wait_recv()
    out_width = pout.shape[1]

    def out_product(start):
        rows = pl.ds(start, R)
        return dot(mixed[rows, :], pout[...].reshape(-1, D))

    res2[...] = core_sum(out_product)
    layer_norm(
        res2, rbuf, res1, second_gain, second_bias, xh2, rs2, n2, pl.multiple_of(place.m * R, 16)
    )
    mine = block(place.m)
    c_n2 = [net.send(n2.at[mine], n2.at[mine], device) for device in (place.far, place.sib)]

    l_cot.wait()
    l_up.wait()
    l_down.wait()
    bias_sum = []

    def feed(m):
        rows = block(m)
        pre = dot(n2[rows, :], up[...]) + up_bias[...].reshape(1, -1)
        value, slope = gelu_parts(pre)
        hid[rows, :] = value.astype(BF16)
        grad = (dot(branch[rows, :], down[...], 1, 1) * slope).astype(BF16)
        preg[rows, :] = grad
        bias_sum.append(jnp.sum(grad.astype(F32), axis=0, keepdims=True))

    def back_part(m):
        return dot(preg[block(m), :], up[...], 1, 1)

    def out_part(m):
        return dot(hid[block(m), :], down[...])

    def mask_branch(m, own_slot):
        rows = block(m)
        start = lax.rem(m, 2) * R
        branch[rows, :] = (
            branch[rows, :].astype(F32) * valid_of(own_slot, start)
        ).astype(BF16)

    mine_far = lax.broadcasted_iota(jnp.int32, (slices, 1), 0) == slot_slice[1 - x]
    far_length = jnp.sum(jnp.where(mine_far, lengths, 0.0), axis=0, keepdims=True)

    def valid_of(own_slot, start):
        at = (lax.broadcasted_iota(jnp.int32, (R, 1), 0) + start).astype(F32)
        return jnp.where(at < (length if own_slot else far_length), 1.0, 0.0)

    c_cot[0].wait_recv()
    f_rows = block(place.far_m)
    c_cot_fwd = net.send(branch.at[f_rows], branch.at[f_rows], place.sib)
    mask_done = []

    mask_branch(place.m, True)
    feed(place.m)
    own[1] = back_part(place.m)
    c_cot[1].wait_recv()
    c_n2[1].wait_recv()
    mask_branch(place.sib_m, True)
    feed(place.sib_m)
    csend[1, 0] = back_part(place.sib_m).astype(BF16)
    c_core = {}
    c_core[1, 0] = net.send(csend.at[1, 0], crecv.at[1, 0], place.sib)
    c_n2[0].wait_recv()
    c_n2_fwd = net.send(n2.at[f_rows], n2.at[f_rows], place.sib)
    csend[0, 0] = out_part(place.sib_m).astype(BF16)
    c_core[0, 0] = net.send(csend.at[0, 0], crecv.at[0, 0], place.sib)
    own[0] = out_part(place.m)
    c_cot_fwd.wait_recv()
    c_n2_fwd.wait_recv()
    mask_branch(place.far_sib_m, False)
    feed(place.far_sib_m)
    csend[1, 1] = back_part(place.far_sib_m).astype(BF16)
    c_core[1, 1] = net.send(csend.at[1, 1], crecv.at[1, 1], place.sib)
    net.sent(c_cot_fwd)
    mask_branch(place.far_m, False)
    feed(place.far_m)
    sbuf[:, 0:D] = back_part(place.far_m)
    c_core[1, 1].wait_recv()
    xsend[1] = (sbuf[:, 0:D] + crecv[1, 1].astype(F32)).astype(BF16)
    c_far = {}
    c_far[1] = net.send(xsend.at[1], xrecv.at[1], place.far)

    def result_send():
        csend[0, 1] = out_part(place.far_sib_m).astype(BF16)
        c_core[0, 1] = net.send(csend.at[0, 1], crecv.at[0, 1], place.sib)
        sbuf[:, 0:D] = out_part(place.far_m)
        c_core[0, 1].wait_recv()
        xsend[0] = (sbuf[:, 0:D] + crecv[0, 1].astype(F32)).astype(BF16)
        c_far[0] = net.send(xsend.at[0], xrecv.at[0], place.far)

    summed = {name: Summed(net, place, AWAY[name], BACK[name], **sums[name]) for name in GRADS}

    def keep(name, slot, at, value):
        ref = sums[name]["grad"]
        rows = ref.shape[-2]
        for t in range(value.shape[0] // rows):
            part = (at + t) // 2, (at + t) % 2
            ref[part if slot is None else (slot,) + part] = value[
                t * rows : (t + 1) * rows
            ].astype(BF16)

    half = D // 2
    for i, name in enumerate(("down0", "down1")):
        keep(name, None, 0, dot(hid[:, i * half : (i + 1) * half], branch[...], 0, 0))
        summed[name].start()
    for i, name in enumerate(("up0", "up1")):
        keep(name, None, 0, dot(n2[:, i * half : (i + 1) * half], preg[...], 0, 0))
        summed[name].start()
    sm[...] = jnp.zeros_like(sm)
    sm[4:5, :] = bias_sum[0] + bias_sum[1] + bias_sum[2] + bias_sum[3]

    def norm_back(grad_of, gain, xh_ref, scale_ref, kept, out_ref, out_start, row):
        gain = gain[...].reshape(1, -1)
        gain_sum = jnp.zeros((1, D), F32)
        bias_total = jnp.zeros((1, D), F32)
        for t in range(3):
            rows = slice(t * step, (t + 1) * step)
            dy, through = grad_of(rows)
            xh = xh_ref[rows, :]
            gain_sum = gain_sum + jnp.sum(dy * xh, axis=0, keepdims=True)
            bias_total = bias_total + jnp.sum(dy, axis=0, keepdims=True)
            dy = dy * gain
            mean_one = jnp.sum(dy, axis=1, keepdims=True) * (1.0 / D)
            mean_two = jnp.sum(dy * xh, axis=1, keepdims=True) * (1.0 / D)
            dx = through + scale_ref[rows, :] * (dy - mean_one - xh * mean_two)
            if kept is not None:
                kept[rows, :] = dx
            out_ref[pl.ds(out_start + t * step, step), :] = dx.astype(BF16)
        sm[row : row + 1, :] = gain_sum
        sm[row + 1 : row + 2, :] = bias_total

    own_part = pl.ds(own_rows, R)
    sg2, eb, sg = res1, mb, act
    copies = {}
    locals_left = []
    tasks = {}

    def task(number):
        def enter(function):
            tasks[number] = function

        return enter

    @task(NORM2)
    def norm2():
        c_core[1, 0].wait_recv()
        c_far[1].wait_recv()

        def grad_of(rows):
            dy = own[1, rows, :] + crecv[1, 0, rows, :].astype(F32) + xrecv[1, rows, :].astype(F32)
            at = pl.ds(pl.multiple_of(place.m * R, 16) + rows.start, step)
            return dy, branch[at, :].astype(F32)

        norm_back(grad_of, second_gain, xh2, rs2, sg2, mb, own_rows, 2)
        copies["mb"] = net.send(mb.at[own_part], mb.at[own_part], place.sib)

    @task(RESULT)
    def result():
        c_core[0, 0].wait_recv()
        c_far[0].wait_recv()
        net.sent(c_core[0, 0])
        for t in range(3):
            rows = slice(t * step, (t + 1) * step)
            value = (
                res2[rows, :]
                + own[0, rows, :]
                + crecv[0, 0, rows, :].astype(F32)
                + xrecv[0, rows, :].astype(F32)
            )
            csend[0, 0, rows, :] = (value * valid_rows(own_rows + t * step, step)).astype(BF16)
        locals_left.append(net.local(csend.at[0, 0], block_out))

    @task(MIXED_BACK)
    def mixed_back():
        copies["mb"].wait_recv()
        value = dot(mixed[...], mb[...], 0, 0)
        shard = pout.shape[1]
        for j in range(2):
            rows = value[j * shard : (j + 1) * shard]
            for i in range(2):
                keep("pout", j, 2 * i, rows[:, i * half : (i + 1) * half])
        for at, size in tile_rows:
            value = dot(mb[at : at + size, :], pout[...].reshape(-1, D), 1, 1).astype(BF16)
            for h in range(2 * per_shard):
                heads[h, at : at + size, :] = value[:, h * HEAD_DIM : (h + 1) * HEAD_DIM]

    def head_back(h, carry):
        p = probs[h]
        dp = dot(heads[h], v[h], 1, 1)
        v[h] = dot(p, heads[h], 0, 0).astype(BF16)
        p = p.astype(F32)
        ds = (p * (dp - jnp.sum(p * dp, axis=1, keepdims=True))).astype(BF16)
        dq = (dot(ds, k[h]) * score_scale).astype(BF16)
        k[h] = (dot(ds, q[h], 0, 0) * score_scale).astype(BF16)
        q[h] = dq
        return carry

    def pin_back(j):
        lax.fori_loop(per_shard * j, per_shard * (j + 1), head_back, 0)

        def store_pg(lanes, value):
            pg[j, :, lanes] = value

        pieces = [ref[per_shard * j + h] for h in range(per_shard) for ref in (q, k, v)]
        side_by_side(pieces, store_pg)
        value = dot(pg[j], n1[...], 0, 0)
        wide = D // 6
        for i in range(6):
            keep("pin%d" % (i // 2), j, 2 * (i % 2), value[:, i * wide : (i + 1) * wide])

    @task(HEADS_FAR)
    def heads_far():
        pin_back(1)

    @task(HEADS_OWN)
    def heads_own():
        pin_back(0)

    @task(NORM1_SEND)
    def norm1_send():
        def product(start):
            rows = pl.ds(start, R)
            return dot(pg[0, rows, :], pin[0]) + dot(pg[1, rows, :], pin[1])

        width = pl.ds(0, D)
        sbuf[:, width] = product(sib_rows)
        copies["n1"] = net.send(sbuf.at[:, width], rbuf.at[:, width], place.sib)
        xh2[...] = product(own_rows)

    @task(NORM1)
    def norm1():
        copies["n1"].wait_recv()
        net.sent(copies["n1"])

        def grad_of(rows):
            return xh2[rows, :] + rbuf[rows, 0:D], sg2[rows, :]

        net.sent(copies["mb"])
        norm_back(grad_of, first_gain, xh1, rs1, None, eb, own_rows, 0)
        copies["eb"] = net.send(eb.at[own_part], eb.at[own_part], place.sib)

    def embed_back(j):
        keep("embed", j, 0, dot(act[j], eb[...], 0, 0))

    cin = feat.shape[1]
    square = pl.ds(0, cin // 4), pl.ds(0, channels)
    spares = [ref.at[square] for ref in (xh1, xh2, res1, own.at[1])]

    def stem_back(j):
        gain_sum = jnp.zeros((1, channels), F32)
        bias_total = jnp.zeros((1, channels), F32)
        for at, size in tile_rows:
            dz = dot(eb[at : at + size, :], embed[j], 1, 1) * dgs[j, at : at + size, :]
            dgs[j, at : at + size, :] = dz
            gain_sum = gain_sum + jnp.sum(dz * xhs[j, at : at + size, :], axis=0, keepdims=True)
            bias_total = bias_total + jnp.sum(dz, axis=0, keepdims=True)
        sm[5 + j : 6 + j, 0:channels] = gain_sum
        sm[5 + j : 6 + j, channels : 2 * channels] = bias_total
        gain = gvec[j, 0:1, :]
        count = 1.0 / (length * GROUP)
        mean_one = group_sum(bias_total * gain) * count
        mean_two = group_sum(gain_sum * gain) * count
        for at, size in tile_rows:
            part = dgs[j, at : at + size, :] * gain - valid_rows(at, size) * (
                mean_one + xhs[j, at : at + size, :] * mean_two
            )
            sg[j, at : at + size, :] = (part * gst[j, 0:1, :]).astype(BF16)
        average, scale = wstat[j, 0:1, :], wstat[j, 1:2, :]
        sum_one = jnp.zeros((1, channels), F32)
        sum_two = jnp.zeros((1, channels), F32)
        quarter = cin // 4
        for t in range(4):
            rows = slice(t * quarter, (t + 1) * quarter)
            grad = dot(feat[:, rows], sg[j], 0, 0)
            spare = spares[t]
            spare[...] = grad
            xh = (stem[j, rows, :].astype(F32) - average) * scale
            sum_one = sum_one + jnp.sum(grad, axis=0, keepdims=True)
            sum_two = sum_two + jnp.sum(grad * xh, axis=0, keepdims=True)
        sum_one = sum_one * (1.0 / cin)
        sum_two = sum_two * (1.0 / cin)
        for t in range(4):
            rows = slice(t * quarter, (t + 1) * quarter)
            xh = (stem[j, rows, :].astype(F32) - average) * scale
            value = (spares[t][...] - sum_one - xh * sum_two) * scale
            for i in range(2):
                lanes = slice(i * channels // 2, (i + 1) * channels // 2)
                keep("stem%d" % i, j, t, value[:, lanes])

    @task(STEM_FAR)
    def stem_far():
        copies["eb"].wait_recv()
        embed_back(1)
        stem_back(1)

    @task(STEM_OWN)
    def stem_own():
        embed_back(0)
        stem_back(0)
        small("core")

    def feature_product(start):
        rows = pl.ds(start, R)
        return dot(sg[0, rows, :], std[0], 1, 1) + dot(sg[1, rows, :], std[1], 1, 1)

    @task(FEATURES_SEND)
    def features_send():
        sbuf[...] = feature_product(sib_rows)
        copies["feat"] = net.send(sbuf, rbuf, place.sib)

    @task(FEATURES_SUM)
    def features_sum():
        copies["feat"].wait_recv()
        net.sent(copies["feat"])
        sbuf[...] = feature_product(own_rows) + rbuf[...]
        locals_left.append(net.local(sbuf, features_grad))

    small_at = {"core": place.sib}
    for name in "xyaw":
        small_at[name] = place.partner(name)[1]
    small_order = tuple(small_at)

    def small(name):
        copies["small"] = net.send(sm, smr.at[small_order.index(name)], small_at[name])

    def small_step(i):
        copies["small"].wait_recv()
        net.sent(copies["small"])
        if small_order[i] in ("core", "x"):
            sm[0:4, :] = sm[0:4, :] + smr[i, 0:4, :]
            if small_order[i] == "x":
                sm[5:6, :] = sm[5:6, :] + smr[i, 6:7, :]
        else:
            sm[...] = sm[...] + smr[i]
        if i + 1 < len(small_order):
            small(small_order[i + 1])
        else:
            o_small[...] = sm[...]

    small_next = list(range(len(small_order)))
    for what in ORDER:
        if what in tasks:
            tasks.pop(what)()
        elif what == SMALL:
            small_step(small_next.pop(0))
        elif what == ~RESULT:
            result_send()
        elif what < 0:
            summed[GRADS[~what]].start()
        else:
            summed[GRADS[what]].step()
    assert not tasks and not small_next
    for one in summed.values():
        one.step_all()
    for copy in locals_left:
        copy.wait()
    net.finish()


def finish(in_names, out_names, *refs):
    names = in_names + out_names
    r = dict(zip(names, refs))
    rest = refs[len(names) :]
    sems, passed, rest = rest[0], rest[1:3], rest[3:]
    held, made = rest[: len(GRADS)], rest[len(GRADS) :]
    made = dict(zip(("up", "down", "pout", "pin", "embed", "stem"), made))
    count = [0]
    going = []

    def move(src, dst):
        copy = pltpu.make_async_copy(src, dst, sems.at[count[0]])
        count[0] += 1
        copy.start()
        return copy

    order = GRADS
    held = dict(zip(GRADS, held))
    as_is = ("block_out", "features_grad")
    passing = [move(r["i_" + name], ref) for name, ref in zip(as_is, passed)]
    arriving = {name: move(r["i_" + name], held[name]) for name in order}
    small = r["i_small"]
    for i, name in enumerate(("g1", "b1", "g2", "b2", "ub")):
        r["o_" + name][...] = small[i, :]
    channels = r["o_gain"].shape[0]
    r["o_gain"][...] = small[5, 0:channels]
    r["o_shift"][...] = small[5, channels : 2 * channels]
    for name, ref, copy in zip(as_is, passed, passing):
        copy.wait()
        going.append(move(ref, r["o_" + name]))
    for name in order:
        arriving[name].wait()
        part = held[name]
        parts, rows, columns = part.shape
        name, number = name.rstrip("012"), int(name[-1]) if name[-1] in "012" else 0
        to = made[name]
        top, left = 0, 0
        if name in ("up", "down"):
            top, down = number * parts * rows, parts
        else:
            down = to.shape[0] // rows
            left = number * (parts // down) * columns
        for t in range(parts):
            at = top + t % down * rows
            lane = left + t // down * columns
            to[at : at + rows, lane : lane + columns] = part[t].astype(F32)
        if name in ("up", "down"):
            rows = pl.ds(top, parts * rows)
            going.append(move(to.at[rows], r["o_" + name].at[rows]))
        elif number == dict(pin=2, stem=1).get(name, 0):
            going.append(move(to, r["o_" + name]))
    for copy in going:
        copy.wait()


def body(
    features, stem_weight, group_gain, group_bias, embed_weight, first_gain, first_bias,
    project_in, project_out, second_gain, second_bias, up_weight, up_bias, down_weight,
    valid_mask, slot_slice, cotangent, *, dp,
):
    slots = slot_slice.shape[0]
    L = features.shape[0] // slots
    R = cotangent.shape[0]
    cin, channels = stem_weight.shape
    D = cotangent.shape[1]
    wide_in = project_in.shape[1]
    project_in = project_in.T
    out_rows = project_out.shape[0]
    hidden = up_weight.shape[1]
    heads = 2 * wide_in // (3 * HEAD_DIM)
    hbm = pl.BlockSpec(memory_space=pl.ANY)
    vmem = pl.BlockSpec(memory_space=pltpu.VMEM)
    smem = pl.BlockSpec(memory_space=pltpu.SMEM)
    in_specs = dict(
        features=hbm, stem_weight=hbm, group_gain=vmem, group_bias=vmem, embed_weight=hbm,
        first_gain=vmem, first_bias=vmem, project_in=hbm, project_out=hbm, second_gain=vmem,
        second_bias=vmem, up_weight=hbm, up_bias=vmem, down_weight=hbm, valid_mask=vmem,
        slot_slice=smem, cotangent=hbm,
    )
    parts = dict(
        up0=(D // 8, hidden),
        up1=(D // 8, hidden),
        down0=(hidden // 8, D),
        down1=(hidden // 8, D),
        pout=(out_rows // 2, D // 2),
        pin0=(wide_in // 2, D // 6),
        pin1=(wide_in // 2, D // 6),
        pin2=(wide_in // 2, D // 6),
        embed=(channels // 4, D),
        stem0=(cin // 4, channels // 2),
        stem1=(cin // 4, channels // 2),
    )
    outs = dict(
        block_out=((R, D), BF16, hbm),
        features_grad=((R, cin), F32, hbm),
        o_small=((8, D), F32, vmem),
    )
    for name in GRADS:
        outs["o_" + name] = ((2, 2) + parts[name], BF16, hbm)
    scratch = dict(
        feat=((L, cin), BF16), stem=((2, cin, channels), BF16), std=((2, cin, channels), BF16),
        wstat=((2, 8, channels), F32), embed=((2, channels, D), BF16), pin=((2, wide_in, D), BF16),
        pout=((2, out_rows, D), BF16), up=((D, hidden), BF16), down=((hidden, D), BF16),
        gvec=((2, 8, channels), F32), xhs=((2, L, channels), F32), dgs=((2, L, channels), F32),
        act=((2, L, channels), BF16), gst=((2, 8, channels), F32),
        sbuf=((R, cin), F32), rbuf=((R, cin), F32), res1=((R, D), F32), xh1=((R, D), F32),
        rs1=((R, 1), F32), n1=((L, D), BF16), q=((heads, L, HEAD_DIM), BF16),
        k=((heads, L, HEAD_DIM), BF16), v=((heads, L, HEAD_DIM), BF16), probs=((heads, L, L), BF16),
        heads=((heads, L, HEAD_DIM), BF16), mixed=((L, heads * HEAD_DIM), BF16),
        res2=((R, D), F32), xh2=((R, D), F32), rs2=((R, 1), F32), n2=((4 * R, D), BF16),
        hid=((4 * R, hidden), BF16), branch=((4 * R, D), BF16), preg=((4 * R, hidden), BF16),
        own=((2, R, D), F32), csend=((2, 2, R, D), BF16),
        crecv=((2, 2, R, D), BF16), xsend=((2, R, D), BF16), xrecv=((2, R, D), BF16),
        mb=((L, D), BF16), pg=((2, L, wide_in), BF16),
    )
    for name in GRADS:
        size = {dim: 2 for dim in "xyb" if dim in AWAY[name]}
        scratch["g_" + name] = (tuple(size.values()) + parts[name], BF16)
        for level, dim in enumerate(AWAY[name]):
            if dim != "a":
                size[dim] = 1
            scratch["r%d_" % level + name] = (tuple(size.values()) + parts[name], BF16)
    scratch.update(sm=((8, D), F32), smr=((5, 8, D), F32))
    copies = 144
    shapes = [pltpu.VMEM(*one) for one in scratch.values()]
    shapes += [pltpu.SemaphoreType.DMA((copies,)) for _ in range(2)]
    shapes += [pltpu.SemaphoreType.DMA((24,))]
    names = tuple(scratch) + ("send_sems", "recv_sems", "local_sems")
    results = pl.pallas_call(
        functools.partial(kernel, tuple(in_specs), tuple(outs), names),
        out_shape=[jax.ShapeDtypeStruct(shape, kind) for shape, kind, _ in outs.values()],
        in_specs=list(in_specs.values()),
        out_specs=[spec for _, _, spec in outs.values()],
        scratch_shapes=shapes,
        compiler_params=pltpu.CompilerParams(
            collective_id=0, has_side_effects=True, vmem_limit_bytes=62 * 2**20
        ),
        name="layer",
    )(
        features, stem_weight, group_gain, group_bias, embed_weight, first_gain, first_bias,
        project_in, project_out, second_gain, second_bias, up_weight, up_bias, down_weight,
        valid_mask, slot_slice, cotangent,
    )
    out = dict(zip(outs, results))

    wide = {name: out["o_" + name].reshape((4,) + parts[name]) for name in GRADS}
    small = out["o_small"]
    bit = NEAR
    if bit < dp:
        wide = {name: part.astype(F32) for name, part in wide.items()}
    while bit < dp:
        pairs = [(i, i ^ bit) for i in range(dp)]
        wide, small = jax.tree.map(
            lambda part: part + lax.ppermute(part, "dp", pairs), (wide, small)
        )
        bit *= 2

    inputs = {"i_" + name: wide[name] for name in GRADS}
    inputs.update(i_block_out=out["block_out"], i_features_grad=out["features_grad"], i_small=small)
    whole = dict(
        up=(D, hidden), down=(hidden, D), pout=(out_rows, D), pin=(wide_in, D),
        embed=(channels, D), stem=(cin, channels),
    )
    finals = dict(o_block_out=((R, D), BF16, hbm), o_features_grad=((R, cin), F32, hbm))
    for name, shape in whole.items():
        finals["o_" + name] = (shape, F32, hbm)
    for name in ("g1", "b1", "g2", "b2"):
        finals["o_" + name] = ((D,), F32, vmem)
    finals["o_ub"] = ((hidden,), F32, vmem)
    for name in ("gain", "shift"):
        finals["o_" + name] = ((channels,), F32, vmem)
    moved = pl.pallas_call(
        functools.partial(finish, tuple(inputs), tuple(finals)),
        out_shape=[jax.ShapeDtypeStruct(shape, kind) for shape, kind, _ in finals.values()],
        in_specs=[hbm] * (len(inputs) - 1) + [vmem],
        out_specs=[spec for _, _, spec in finals.values()],
        scratch_shapes=[pltpu.SemaphoreType.DMA((28,))]
        + [pltpu.VMEM((R, D), BF16), pltpu.VMEM((R, cin), F32)]
        + [pltpu.VMEM(wide[name].shape, wide[name].dtype) for name in GRADS]
        + [pltpu.VMEM(shape, F32) for shape in whole.values()],
        compiler_params=pltpu.CompilerParams(vmem_limit_bytes=62 * 2**20),
        name="finish",
    )(*inputs.values())
    done = dict(zip(finals, moved))
    return (
        done["o_block_out"],
        done["o_features_grad"],
        done["o_stem"],
        done["o_gain"],
        done["o_shift"],
        done["o_embed"],
        done["o_g1"],
        done["o_b1"],
        done["o_pin"].T,
        done["o_pout"],
        done["o_g2"],
        done["o_b2"],
        done["o_up"],
        done["o_ub"],
        done["o_down"],
    )


def solution(mesh):
    return jax.shard_map(
        functools.partial(body, dp=mesh.shape["dp"]),
        mesh=mesh,
        in_specs=(
            P("dp", None), P(None, "mp"), P("mp"), P("mp"), P("mp", None), P(), P(),
            P(None, "mp"), P("mp", None), P(), P(), P(None, "mp"), P("mp"), P("mp", None),
            P(), P("dp"), P(("dp", "mp"), None),
        ),
        out_specs=(
            P(("dp", "mp"), None), P(("dp", "mp"), None), P(None, "mp"), P("mp"), P("mp"),
            P("mp", None), P(), P(), P(None, "mp"), P("mp", None), P(), P(), P(None, "mp"),
            P("mp"), P("mp", None),
        ),
        check_vma=False,
    )
```

profile of v0, /device:TPU:0, one launch (start us, length us, event | category | flops | bytes accessed | tf_op | source)
XLA Modules:
  0.0 172.8 jit_solution(3092051858949035093)
XLA Ops:
  0.7 165.0 %layer.1 = (bf16[288,768]{1,0:T(8,128)(2,1)}, f32[288,1024]{1,0:T(8,128)}, f32[8,768]{1,0:T(8,128)}, bf16[2,2,96,768]{3,2,1,0:T(8,128)(2,1)}, bf16[2,2,96,768]{3...) custom-call(bf16[1152,1024]{1,0:T(8,128)(2,1)} %refs_0_.1, ...), custom_call_target="tpu_custom_call" | custom-call | tf_op jit(solution)/shard_map/layer/pallas_call | solution.py:980
  165.7 6.9 %finish.1 = (bf16[288,768]{1,0:T(8,128)(2,1)}, f32[288,1024]{1,0:T(8,128)}, f32[768,768]{1,0:T(8,128)}, f32[768,768]{1,0:T(8,128)}, f32[192,768]{1,0:T(8,128)}, ...) custom-call(bf16[4,96,768]{2,1,0:T(8,128)(2,1)} %bitcast.14, ...), custom_call_target="tpu_custom_call" | custom-call | tf_op jit(solution)/shard_map/finish/pallas_call | solution.py:1023
where the time goes:
time: 173 us
  Pallas kernels  172 us (99%)
    pallas_call x1, Pallas kernels, body(): pl.pallas_call(functools.partial(kernel, tuple(in_specs), tuple(outs), na...  165 us
    pallas_call x1, Pallas kernels, body(): pl.pallas_call(functools.partial(finish, tuple(inputs), tuple(finals)), o...  6.88 us

commit v1 on v0

--- a/solution.py
+++ b/solution.py
@@ -394,9 +394,8 @@
     c_embed.wait_recv()
 
     def core_sum(product):
-        width = pl.ds(0, D)
-        sbuf[:, width] = product(sib_rows)
-        copy = net.send(sbuf.at[:, width], rbuf.at[:, width], place.sib)
+        xsend[0] = product(sib_rows).astype(BF16)
+        copy = net.send(xsend.at[0], xrecv.at[0], place.sib)
         mine = product(own_rows)
         copy.wait_recv()
         net.sent(copy)
@@ -408,13 +407,13 @@
 
     res1[...] = core_sum(embed_product)
 
-    step = R // 3
-
-    def layer_norm(res, other, add, gain, bias, xh_ref, scale_ref, out_ref, out_start):
+    step = R // 2
+
+    def layer_norm(res, other, add, gain, bias, xh_ref, scale_ref, out_ref, out_start, made):
         gain, bias = gain[...].reshape(1, -1), bias[...].reshape(1, -1)
-        for t in range(3):
+        for t in range(2):
             rows = slice(t * step, (t + 1) * step)
-            value = res[rows, :] + other[rows, 0:D]
+            value = res[rows, :] + other[rows, :].astype(F32)
             if add is not None:
                 value = value + add[rows, :]
             res[rows, :] = value
@@ -424,9 +423,13 @@
             xh = value * scale
             xh_ref[rows, :] = xh
             scale_ref[rows, :] = scale
-            out_ref[pl.ds(out_start + t * step, step), :] = (xh * gain + bias).astype(BF16)
-
-    layer_norm(res1, rbuf, None, first_gain, first_bias, xh1, rs1, n1, own_rows)
+            at = pl.ds(out_start + t * step, step)
+            out_ref[at, :] = (xh * gain + bias).astype(BF16)
+            made(at)
+
+    layer_norm(
+        res1, xrecv.at[0], None, first_gain, first_bias, xh1, rs1, n1, own_rows, lambda at: None
+    )
     c_n1 = net.send(n1.at[pl.ds(own_rows, R)], n1.at[pl.ds(own_rows, R)], place.sib)
     l_pin.wait()
     c_n1.wait_recv()
@@ -497,28 +500,32 @@
         return dot(mixed[rows, :], pout[...].reshape(-1, D))
 
     res2[...] = core_sum(out_product)
+    c_n2 = []
     layer_norm(
-        res2, rbuf, res1, second_gain, second_bias, xh2, rs2, n2, pl.multiple_of(place.m * R, 16)
+        res2, xrecv.at[0], res1, second_gain, second_bias, xh2, rs2, n2,
+        pl.multiple_of(place.m * R, 16),
+        lambda at: c_n2.append(net.send(n2.at[at], n2.at[at], place.far)),
     )
     mine = block(place.m)
-    c_n2 = [net.send(n2.at[mine], n2.at[mine], device) for device in (place.far, place.sib)]
+    c_n2_sib = net.send(n2.at[mine], n2.at[mine], place.sib)
 
     l_cot.wait()
     l_up.wait()
     l_down.wait()
-    bias_sum = []
-
-    def feed(m):
-        rows = block(m)
+    sm[...] = jnp.zeros_like(sm)
+
+    def part(m, t):
+        return pl.ds(pl.multiple_of(m * R + t * step, 16), step)
+
+    def feed(m, t):
+        rows = part(m, t)
         pre = dot(n2[rows, :], up[...]) + up_bias[...].reshape(1, -1)
         value, slope = gelu_parts(pre)
         hid[rows, :] = value.astype(BF16)
         grad = (dot(branch[rows, :], down[...], 1, 1) * slope).astype(BF16)
         preg[rows, :] = grad
-        bias_sum.append(jnp.sum(grad.astype(F32), axis=0, keepdims=True))
-
-    def back_part(m):
-        return dot(preg[block(m), :], up[...], 1, 1)
+        sm[4:5, :] = sm[4:5, :] + jnp.sum(grad.astype(F32), axis=0, keepdims=True)
+        return dot(grad, up[...], 1, 1)
 
     def out_part(m):
         return dot(hid[block(m), :], down[...])
@@ -540,37 +547,61 @@
     c_cot[0].wait_recv()
     f_rows = block(place.far_m)
     c_cot_fwd = net.send(branch.at[f_rows], branch.at[f_rows], place.sib)
-    mask_done = []
-
     mask_branch(place.m, True)
-    feed(place.m)
-    own[1] = back_part(place.m)
-    c_cot[1].wait_recv()
-    c_n2[1].wait_recv()
-    mask_branch(place.sib_m, True)
-    feed(place.sib_m)
-    csend[1, 0] = back_part(place.sib_m).astype(BF16)
+
+    def feed_near(i, carry):
+        t = lax.rem(i, 2)
+
+        @pl.when(i == 2)
+        def _():
+            c_cot[1].wait_recv()
+            c_n2_sib.wait_recv()
+            mask_branch(place.sib_m, True)
+
+        term = feed(jnp.where(i < 2, place.m, place.sib_m), t)
+        rows = pl.ds(pl.multiple_of(t * step, 16), step)
+
+        @pl.when(i < 2)
+        def _():
+            own[1, rows, :] = term
+
+        @pl.when(i >= 2)
+        def _():
+            csend[1, 0, rows, :] = term.astype(BF16)
+
+        return carry
+
+    lax.fori_loop(0, 4, feed_near, 0)
     c_core = {}
     c_core[1, 0] = net.send(csend.at[1, 0], crecv.at[1, 0], place.sib)
-    c_n2[0].wait_recv()
-    c_n2_fwd = net.send(n2.at[f_rows], n2.at[f_rows], place.sib)
     csend[0, 0] = out_part(place.sib_m).astype(BF16)
     c_core[0, 0] = net.send(csend.at[0, 0], crecv.at[0, 0], place.sib)
     own[0] = out_part(place.m)
     c_cot_fwd.wait_recv()
-    c_n2_fwd.wait_recv()
+    net.sent(c_cot_fwd)
     mask_branch(place.far_sib_m, False)
-    feed(place.far_sib_m)
-    csend[1, 1] = back_part(place.far_sib_m).astype(BF16)
-    c_core[1, 1] = net.send(csend.at[1, 1], crecv.at[1, 1], place.sib)
-    net.sent(c_cot_fwd)
     mask_branch(place.far_m, False)
-    feed(place.far_m)
-    sbuf[:, 0:D] = back_part(place.far_m)
-    c_core[1, 1].wait_recv()
-    xsend[1] = (sbuf[:, 0:D] + crecv[1, 1].astype(F32)).astype(BF16)
     c_far = {}
-    c_far[1] = net.send(xsend.at[1], xrecv.at[1], place.far)
+
+    def feed_far(t):
+        rows = pl.ds(t * step, step)
+        c_n2[t].wait_recv()
+        passed = n2.at[part(place.far_m, t)]
+        passing = net.send(passed, passed, place.sib)
+        sbuf[rows, 0:D] = feed(place.far_m, t)
+        passing.wait_recv()
+        csend[1, 1, rows, :] = feed(place.far_sib_m, t).astype(BF16)
+        c_core[1, 1, t] = net.send(csend.at[1, 1, rows], crecv.at[1, 1, rows], place.sib)
+
+    def feed_return(t):
+        rows = pl.ds(t * step, step)
+        c_core[1, 1, t].wait_recv()
+        xsend[1, rows, :] = (sbuf[rows, 0:D] + crecv[1, 1, rows, :].astype(F32)).astype(BF16)
+        c_far[1, t] = net.send(xsend.at[1, rows], xrecv.at[1, rows], place.far)
+
+    feed_far(0)
+    feed_return(0)
+    feed_far(1)
 
     def result_send():
         csend[0, 1] = out_part(place.far_sib_m).astype(BF16)
@@ -595,17 +626,17 @@
     for i, name in enumerate(("down0", "down1")):
         keep(name, None, 0, dot(hid[:, i * half : (i + 1) * half], branch[...], 0, 0))
         summed[name].start()
+        if i == 0:
+            feed_return(1)
     for i, name in enumerate(("up0", "up1")):
         keep(name, None, 0, dot(n2[:, i * half : (i + 1) * half], preg[...], 0, 0))
         summed[name].start()
-    sm[...] = jnp.zeros_like(sm)
-    sm[4:5, :] = bias_sum[0] + bias_sum[1] + bias_sum[2] + bias_sum[3]
 
     def norm_back(grad_of, gain, xh_ref, scale_ref, kept, out_ref, out_start, row):
         gain = gain[...].reshape(1, -1)
         gain_sum = jnp.zeros((1, D), F32)
         bias_total = jnp.zeros((1, D), F32)
-        for t in range(3):
+        for t in range(2):
             rows = slice(t * step, (t + 1) * step)
             dy, through = grad_of(rows)
             xh = xh_ref[rows, :]
@@ -636,9 +667,9 @@
     @task(NORM2)
     def norm2():
         c_core[1, 0].wait_recv()
-        c_far[1].wait_recv()
 
         def grad_of(rows):
+            c_far[1, rows.start // step].wait_recv()
             dy = own[1, rows, :] + crecv[1, 0, rows, :].astype(F32) + xrecv[1, rows, :].astype(F32)
             at = pl.ds(pl.multiple_of(place.m * R, 16) + rows.start, step)
             return dy, branch[at, :].astype(F32)
@@ -651,7 +682,7 @@
         c_core[0, 0].wait_recv()
         c_far[0].wait_recv()
         net.sent(c_core[0, 0])
-        for t in range(3):
+        for t in range(2):
             rows = slice(t * step, (t + 1) * step)
             value = (
                 res2[rows, :]

time: 173 us -> 168 us (0.971)
  Pallas kernels: 172 us -> 167 us
    pallas_call x1, Pallas kernels: 165 us -> 160 us  [body(): pl.pallas_call(functools.partial(kernel, tuple(in_specs), tuple(outs), na...]
where the time goes in v1:
time: 168 us; the launch traced here: 167 us
  Pallas kernels  167 us (99%)
    pallas_call x1, Pallas kernels, body(): pl.pallas_call(functools.partial(kernel, tuple(in_specs), tuple(outs), na...  160 us
    pallas_call x1, Pallas kernels, body(): pl.pallas_call(functools.partial(finish, tuple(inputs), tuple(finals)), o...  6.88 us

profile of v1, /device:TPU:0, one launch (start us, length us, event | category | flops | bytes accessed | tf_op | source)
XLA Modules:
  0.0 167.4 jit_solution(4291074341308279054)
XLA Ops:
  0.7 159.7 %layer.1 = (bf16[288,768]{1,0:T(8,128)(2,1)}, f32[288,1024]{1,0:T(8,128)}, f32[8,768]{1,0:T(8,128)}, bf16[2,2,96,768]{3,2,1,0:T(8,128)(2,1)}, bf16[2,2,96,768]{3...) custom-call(bf16[1152,1024]{1,0:T(8,128)(2,1)} %refs_0_.1, ...), custom_call_target="tpu_custom_call" | custom-call | tf_op jit(solution)/shard_map/layer/pallas_call | solution.py:1011
  160.3 6.9 %finish.1 = (bf16[288,768]{1,0:T(8,128)(2,1)}, f32[288,1024]{1,0:T(8,128)}, f32[768,768]{1,0:T(8,128)}, f32[768,768]{1,0:T(8,128)}, f32[192,768]{1,0:T(8,128)}, ...) custom-call(bf16[4,96,768]{2,1,0:T(8,128)(2,1)} %bitcast.14, ...), custom_call_target="tpu_custom_call" | custom-call | tf_op jit(solution)/shard_map/finish/pallas_call | solution.py:1054

commit v2 on v1

--- a/solution.py
+++ b/solution.py
@@ -198,46 +198,50 @@
         return bit, (self.d + stride - 2 * stride * bit, self.m)
 
 
-GRADS = ("up0", "up1", "down0", "down1", "pout", "pin0", "pin1", "pin2", "embed", "stem0", "stem1")
-UP0, UP1, DOWN0, DOWN1, POUT, PIN0, PIN1, PIN2, EMBED, STEM0, STEM1, SMALL = range(12)
+GRADS = ("up0", "up1", "up2", "down0", "down1", "down2", "pout", "pin0", "pin1", "pin2", "embed", "stem0", "stem1")
+UP0, UP1, UP2, DOWN0, DOWN1, DOWN2, POUT, PIN0, PIN1, PIN2, EMBED, STEM0, STEM1, SMALL = range(14)
 (NORM2, RESULT, MIXED_BACK, HEADS_FAR, HEADS_OWN, NORM1_SEND, NORM1, STEM_FAR, STEM_OWN, FEATURES_SEND,
- FEATURES_SUM) = range(12, 23)
+ FEATURES_SUM) = range(14, 25)
 KINDS = dict(g="grad", o="out", r0="arrive0", r1="arrive1", r2="arrive2", r3="arrive3")
 AWAY = dict(
     down0="yab",
-    down1="aby",
-    up0="yab",
+    down1="yab",
+    down2="yab",
+    up0="aby",
     up1="yab",
-    pout="xaby",
+    up2="yab",
+    pout="yxab",
     pin0="xaby",
-    pin1="yxab",
-    pin2="yxab",
-    embed="xaby",
-    stem0="xaby",
+    pin1="xaby",
+    pin2="xyab",
+    embed="xyab",
+    stem0="xyab",
     stem1="xyab",
 )
 BACK = dict(
     down0="bay",
-    down1="yba",
-    up0="bay",
-    up1="bay",
+    down1="bay",
+    down2="bay",
+    up0="yba",
+    up1="yba",
+    up2="bay",
     pout="bay",
     pin0="bay",
     pin1="bay",
-    pin2="bya",
+    pin2="bay",
     embed="bay",
-    stem0="bay",
+    stem0="yba",
     stem1="bay",
 )
 ORDER = (
-    NORM2, ~RESULT, DOWN0, MIXED_BACK, HEADS_FAR, ~POUT, DOWN1, UP0, HEADS_OWN, ~PIN1, DOWN0, UP1,
-    NORM1_SEND, DOWN1, UP0, NORM1, ~PIN0, ~PIN2, POUT, DOWN0, STEM_FAR, ~STEM0, ~EMBED, PIN1, UP1,
-    UP0, STEM_OWN, ~STEM1, DOWN1, DOWN0, FEATURES_SEND, SMALL, PIN0, POUT, UP1, FEATURES_SUM, PIN2,
-    RESULT, UP0, STEM0, DOWN1, PIN0, POUT, DOWN0, UP1, STEM0, EMBED, UP0, PIN1, DOWN0, DOWN1, POUT,
-    PIN0, UP1, STEM1, SMALL, EMBED, STEM0, UP0, POUT, PIN2, PIN1, PIN0, UP1, PIN2, EMBED, PIN1,
-    STEM1, SMALL, DOWN1, STEM0, PIN0, PIN2, POUT, PIN1, EMBED, STEM0, SMALL, STEM1, PIN0, PIN2,
-    POUT, PIN1, EMBED, STEM1, STEM0, PIN0, SMALL, STEM1, PIN1, PIN2, EMBED, STEM0, STEM1, EMBED,
-    STEM1, PIN2,
+    NORM2, ~RESULT, DOWN0, MIXED_BACK, ~POUT, DOWN1, UP0, HEADS_FAR, ~PIN2, DOWN2, DOWN0,
+    HEADS_OWN, ~PIN0, UP1, UP0, DOWN1, UP2, DOWN0, DOWN2, NORM1_SEND, ~PIN1, PIN2, POUT, DOWN1,
+    UP1, NORM1, UP0, DOWN0, STEM_FAR, ~EMBED, DOWN2, UP2, PIN0, PIN2, DOWN1, UP0, UP1, STEM_OWN,
+    ~STEM0, DOWN0, PIN1, DOWN2, SMALL, FEATURES_SEND, UP2, POUT, PIN0, DOWN1, FEATURES_SUM, ~STEM1,
+    RESULT, DOWN0, UP0, PIN2, UP1, DOWN2, UP2, DOWN1, EMBED, PIN0, PIN1, PIN2, DOWN2, POUT, STEM0,
+    SMALL, UP1, UP0, EMBED, PIN1, PIN0, UP2, PIN2, STEM1, POUT, STEM0, SMALL, PIN0, PIN1, EMBED,
+    POUT, UP2, STEM0, UP1, PIN1, STEM1, EMBED, PIN2, SMALL, STEM0, PIN0, STEM1, EMBED, PIN2, POUT,
+    STEM1, STEM0, PIN0, PIN1, SMALL, POUT, STEM1, EMBED, STEM0, PIN1, STEM1, EMBED, STEM0, STEM1,
 )
 
 
@@ -623,13 +627,15 @@
             ].astype(BF16)
 
     half = D // 2
-    for i, name in enumerate(("down0", "down1")):
-        keep(name, None, 0, dot(hid[:, i * half : (i + 1) * half], branch[...], 0, 0))
+    third = hid.shape[1] // 3
+    for i, name in enumerate(("down0", "down1", "down2")):
+        keep(name, None, 0, dot(hid[:, i * third : (i + 1) * third], branch[...], 0, 0))
         summed[name].start()
         if i == 0:
             feed_return(1)
-    for i, name in enumerate(("up0", "up1")):
-        keep(name, None, 0, dot(n2[:, i * half : (i + 1) * half], preg[...], 0, 0))
+    third = D // 3
+    for i, name in enumerate(("up0", "up1", "up2")):
+        keep(name, None, 0, dot(n2[:, i * third : (i + 1) * third], preg[...], 0, 0))
         summed[name].start()
 
     def norm_back(grad_of, gain, xh_ref, scale_ref, kept, out_ref, out_start, row):
@@ -960,10 +966,12 @@
         slot_slice=smem, cotangent=hbm,
     )
     parts = dict(
-        up0=(D // 8, hidden),
-        up1=(D // 8, hidden),
-        down0=(hidden // 8, D),
-        down1=(hidden // 8, D),
+        up0=(D // 12, hidden),
+        up1=(D // 12, hidden),
+        up2=(D // 12, hidden),
+        down0=(hidden // 12, D),
+        down1=(hidden // 12, D),
+        down2=(hidden // 12, D),
         pout=(out_rows // 2, D // 2),
         pin0=(wide_in // 2, D // 6),
         pin1=(wide_in // 2, D // 6),
@@ -1003,10 +1011,10 @@
                 size[dim] = 1
             scratch["r%d_" % level + name] = (tuple(size.values()) + parts[name], BF16)
     scratch.update(sm=((8, D), F32), smr=((5, 8, D), F32))
-    copies = 144
+    copies = 168
     shapes = [pltpu.VMEM(*one) for one in scratch.values()]
     shapes += [pltpu.SemaphoreType.DMA((copies,)) for _ in range(2)]
-    shapes += [pltpu.SemaphoreType.DMA((24,))]
+    shapes += [pltpu.SemaphoreType.DMA((32,))]
     names = tuple(scratch) + ("send_sems", "recv_sems", "local_sems")
     results = pl.pallas_call(
         functools.partial(kernel, tuple(in_specs), tuple(outs), names),
@@ -1056,7 +1064,7 @@
         out_shape=[jax.ShapeDtypeStruct(shape, kind) for shape, kind, _ in finals.values()],
         in_specs=[hbm] * (len(inputs) - 1) + [vmem],
         out_specs=[spec for _, _, spec in finals.values()],
-        scratch_shapes=[pltpu.SemaphoreType.DMA((28,))]
+        scratch_shapes=[pltpu.SemaphoreType.DMA((40,))]
         + [pltpu.VMEM((R, D), BF16), pltpu.VMEM((R, cin), F32)]
         + [pltpu.VMEM(wide[name].shape, wide[name].dtype) for name in GRADS]
         + [pltpu.VMEM(shape, F32) for shape in whole.values()],

time: 168 us -> 167 us (level)
  no operation moved by 1% of the time
where the time goes in v2:
time: 167 us
  Pallas kernels  166 us (99%)
    pallas_call x1, Pallas kernels, body(): pl.pallas_call(functools.partial(kernel, tuple(in_specs), tuple(outs), na...  159 us
    pallas_call x1, Pallas kernels, body(): pl.pallas_call(functools.partial(finish, tuple(inputs), tuple(finals)), o...  7 us

profile of v2, /device:TPU:0, one launch (start us, length us, event | category | flops | bytes accessed | tf_op | source)
XLA Modules:
  0.0 167.0 jit_solution(2364879539999211816)
XLA Ops:
  0.7 159.1 %layer.1 = (bf16[288,768]{1,0:T(8,128)(2,1)}, f32[288,1024]{1,0:T(8,128)}, f32[8,768]{1,0:T(8,128)}, bf16[2,2,64,768]{3,2,1,0:T(8,128)(2,1)}, bf16[2,2,64,768]{3...) custom-call(bf16[1152,1024]{1,0:T(8,128)(2,1)} %refs_0_.1, ...), custom_call_target="tpu_custom_call" | custom-call | tf_op jit(solution)/shard_map/layer/pallas_call | solution.py:1019
  159.8 7.0 %finish.1 = (bf16[288,768]{1,0:T(8,128)(2,1)}, f32[288,1024]{1,0:T(8,128)}, f32[768,768]{1,0:T(8,128)}, f32[768,768]{1,0:T(8,128)}, f32[192,768]{1,0:T(8,128)}, ...) custom-call(bf16[4,64,768]{2,1,0:T(8,128)(2,1)} %bitcast.16, ...), custom_call_target="tpu_custom_call" | custom-call | tf_op jit(solution)/shard_map/finish/pallas_call | solution.py:1062
